TPU v7x, 32 devices: a whole 2x2x4 slice. The times are simulated.
32 devices in a mesh: group: 2 (over y), pool: 2 (over core), dev: 8 (over z, x).
Axes of the slice: x: 2, y: 2, z: 4, core: 2. Of those that a mesh axis runs over, the one named last changes fastest.
Arguments:
- tokens: bfloat16 [2, 1024, 7168], P(None, ('group', 'pool', 'dev')), parts along dimension 1, may hold values from -6 to 6
- routes: int32 [2, 1024, 8], P(None, ('group', 'pool', 'dev')), parts along dimension 1, may hold values from 0 to 255, all different within a row; in each aligned block of 32 rows (0 to 31, 32 to 63, ..., all dimensions but the last counted through in order) at most 2 rows name the same one
- router: bfloat16 [256, 7168], P(('pool', 'dev')), may hold values from -0.0625 to 0.0625
- w_gate: bfloat16 [7168, 4096], P(None, ('pool', 'dev')), may hold values from -0.0625 to 0.0625
- w_up: bfloat16 [7168, 4096], P(None, ('pool', 'dev')), may hold values from -0.0625 to 0.0625
- w_down: bfloat16 [4096, 7168], P(('pool', 'dev')), may hold values from -0.125 to 0.125
Outputs:
- combined: bfloat16 [2, 1024, 7168], P(None, ('group', 'pool', 'dev')), parts along dimension 1
There are 2 independent parts, one for each index of `group`. A program takes and returns all parts, laid end to end along the dimension named above; an argument that names none is the same for every part. Nothing has to cross between parts.
Inputs may be any that keep to these rules, and one draw needn't show every extreme that they name: `routes`: each row names 8 different experts; in each micro-batch the rows of one device name no expert more than 2 times, a bound that some block reaches.
All inputs are finite; a program needn't handle non-finite values.
Results may differ from a plain program's by a relative error of at most 0.009.
Values may be sent and summed in bfloat16 or wider, within the bound.
A program may use at most 128 MiB of HBM per device.

v0:
```python
import jax
import jax.numpy as jnp
from jax import lax
from jax.sharding import PartitionSpec as P

FF = 2048
CAP = 2


route_scale = 2.5


def per_device(tokens, routes, router, w_gate, w_up, w_down):
    groups = lax.axis_size(("pool", "dev"))
    batches = tokens.shape[0]
    model_width = tokens.shape[2]
    hidden_width = w_gate.shape[1]
    slices = FF // hidden_width
    experts_win = groups // slices
    capacity = CAP
    logits = jnp.einsum(
        "mrd,ed->mre",
        tokens,
        lax.all_gather(router, ("pool", "dev"), axis=0, tiled=True),
        preferred_element_type=jnp.float32,
    )
    scores = jax.nn.sigmoid(logits)
    expert_ids = jnp.arange(logits.shape[2], dtype=jnp.int32)
    picked = routes[..., None] == expert_ids
    chosen = jnp.sum(jnp.where(picked, scores[:, :, None, :], 0.0), axis=-1)
    weights = route_scale * chosen / jnp.sum(chosen, axis=-1, keepdims=True)
    window = picked[..., :experts_win]
    route_weight = jnp.sum(jnp.where(window, weights[..., None], 0.0), axis=2)
    routed = jnp.any(window, axis=2).astype(jnp.int32)
    position = jnp.cumsum(routed, axis=1) - 1
    slot_ids = jnp.arange(capacity, dtype=jnp.int32)
    selector = (routed[..., None] == 1) & (position[..., None] == slot_ids)
    slot_rows = jnp.einsum(
        "mrec,mrd->mecd", selector.astype(jnp.bfloat16), tokens, preferred_element_type=jnp.float32
    ).astype(jnp.bfloat16)
    outgoing = jnp.broadcast_to(
        slot_rows[:, :, None], (batches, experts_win, slices, capacity, model_width)
    )
    outgoing = outgoing.reshape(batches, groups, capacity, model_width)
    arrived = lax.all_to_all(outgoing, ("pool", "dev"), split_axis=1, concat_axis=1, tiled=True)
    flat_rows = arrived.reshape(-1, model_width)
    gate_proj = jnp.dot(flat_rows, w_gate, preferred_element_type=jnp.float32)
    up_proj = jnp.dot(flat_rows, w_up, preferred_element_type=jnp.float32)
    hidden = (jax.nn.silu(gate_proj) * up_proj).astype(jnp.bfloat16)
    partial_value = jnp.dot(hidden, w_down, preferred_element_type=jnp.float32).astype(jnp.bfloat16)
    send_partial_value = partial_value.reshape(arrived.shape)
    returned = lax.all_to_all(
        send_partial_value, ("pool", "dev"), split_axis=1, concat_axis=1, tiled=True
    )
    returned = returned.reshape(batches, experts_win, slices, capacity, model_width)
    expert_out = jnp.sum(returned, axis=2, dtype=jnp.float32)
    mixing = selector.astype(jnp.float32) * route_weight[..., None]
    combined = jnp.einsum("mrec,mecd->mrd", mixing, expert_out, precision=lax.Precision.HIGHEST)
    return combined.astype(jnp.bfloat16)


def solution(mesh):
    placed = (
        P(None, ("group", "pool", "dev"), None),
        P(None, ("group", "pool", "dev"), None),
        P(("pool", "dev"), None),
        P(None, ("pool", "dev")),
        P(None, ("pool", "dev")),
        P(("pool", "dev"), None),
    )
    return jax.shard_map(
        per_device,
        mesh=mesh,
        in_specs=placed,
        out_specs=P(None, ("group", "pool", "dev"), None),
        check_vma=False,
    )
```

profile of v0, /device:TPU:1, one launch (start us, length us, event | category | flops | bytes accessed | tf_op | source)
XLA Modules:
  0.0 100.5 jit_solution(16834733776475788198)
XLA Ops:
  6.5 0.0 copy-start
  6.5 0.0 all-gather.2.cloned.1.call-start
  6.5 0.7 all-gather.2.cloned.1.call-update
  7.3 1.0 iota_compare_fusion
  8.3 0.1 copy.40
  8.4 0.1 reduce_window_sum.11
  8.4 0.1 copy.41
  8.5 0.0 copy-done
  8.5 0.2 convolution_convert_fusion.1
  8.8 0.1 copy.47
  8.9 0.5 broadcast_in_dim.43
  9.4 37.5 %all_to_all.10 = bf16[2,16,2,7168]{3,2,0,1:T(2,128)(2,1)S(1)} all-to-all(bf16[2,16,2,7168]{3,2,0,1:T(2,128)(2,1)S(1)} %bitcast.31), channel_id=1, replica_groups=mesh['group'=2,'pool'=2,'dev'=8] {'pool','dev'}, dimensions={1} | all-to-all | bytes 1835008 | tf_op jit(solution)/shard_map/all_to_all | solution.py:45
  46.8 0.6 copy.48
  47.5 0.3 reshape.36
  47.8 2.8 %fusion.31 = f32[64,256]{1,0:T(8,128)S(1)} fusion(bf16[64,7168]{1,0:T(8,128)(2,1)S(1)} %reshape.36, bf16[7168,256]{1,0:T(8,128)(2,1)} %param.9), kind=kOutput, calls=%fused_computation.37 | convolution fusion | flops 234881024 | bytes 4653056 | tf_op jit(solution)/shard_map/dot_general | solution.py:47
  50.6 5.5 %convolution_convert_fusion = bf16[64,7168]{1,0:T(8,128)(2,1)S(1)} fusion(bf16[256,7168]{1,0:T(8,128)(2,1)} %param.11, bf16[64,7168]{1,0:T(8,128)(2,1)S(1)} %reshape.36, bf16[7168,256]{1,0:T(8,128)(2,1)} %param.10, f32[64,256]{1,0:T(8,128)S(1)} %fusion.31), kind=kOutput, calls=%fused_computation.2 | convolution fusion | flops 470319104 | bytes 9240576 | tf_op jit(solution)/shard_map/dot_general | solution.py:50
  56.1 0.3 reshape.37
  56.4 0.6 copy.49
  57.1 0.0 copy-start.1
  57.1 29.2 %all_to_all.11 = bf16[2,16,2,7168]{3,2,0,1:T(2,128)(2,1)S(1)} all-to-all(bf16[2,16,2,7168]{3,2,0,1:T(2,128)(2,1)S(1)} %copy.49), channel_id=1, replica_groups=mesh['group'=2,'pool'=2,'dev'=8] {'pool','dev'}, dimensions={1} | all-to-all | bytes 1835008 | tf_op jit(solution)/shard_map/all_to_all | solution.py:52
  86.3 0.8 convert_reduce_fusion
  87.2 0.0 all-gather.2.cloned.1.call-done
  87.2 3.3 %fusion.12 = f32[2,32,256]{2,1,0:T(8,128)S(1)} fusion(bf16[2,32,7168]{2,1,0:T(8,128)(2,1)S(1)} %copy-done, bf16[256,7168]{1,0:T(8,128)(2,1)} %all-gather.2.cloned.1.call-done), kind=kOutput, calls=%fused_computation.13 | convolution fusion | flops 234930176 | bytes 4653056 | tf_op jit(solution)/shard_map/mrd,ed->mre/dot_general | solution.py:21
  90.5 0.1 copy.42
  90.6 0.0 copy-done.1
  90.6 0.3 select_reduce_fusion.1
  90.9 2.7 %fusion = bf16[2,32,7168]{2,1,0:T(8,128)(2,1)} fusion(f32[2,2,2,7168]{3,2,0,1:T(2,128)S(1)} %convert_reduce_fusion, pred[2,32,2,2]{1,2,3,0:T(4,128)(4,1)S(1)} %compare_and_fusion, f32[2,32,2]{1,2,0:T(2,128)S(1)} %select_reduce_fusion.2), kind=kOutput, calls=%fused_computation.1 | convolution fusion | flops 22479104 | bytes 1147648 | tf_op jit(solution)/shard_map/mrec,mecd->mrd/dot_general | solution.py:58
  (6 shorter events, 0.1 us)
Async XLA Ops:
  6.5 2.0 %copy-start = (bf16[2,32,7168]{2,1,0:T(8,128)(2,1)S(1)}, bf16[2,32,7168]{2,1,0:T(8,128)(2,1)}, u32[]{:S(2)}) copy-start(bf16[2,32,7168]{2,1,0:T(8,128)(2,1)} %param.6) | copy-start | bytes 2752516
  6.5 80.6 %all-gather.2.cloned.1.call-start = ((), (), s32[]{:S(2)}) async-start(), calls=%async_computation.2 | async-start | bytes 3899392 | tf_op jit(solution)/shard_map/all_gather | solution.py:24
  57.1 33.5 %copy-start.1 = (s32[2,32,8]{1,2,0:T(8,128)S(1)}, s32[2,32,8]{1,2,0:T(8,128)}, u32[]{:S(2)}) copy-start(s32[2,32,8]{1,2,0:T(8,128)} %param.7) | copy-start | bytes 6148
Sparse Core Ops, SparseCore 0:
  9.6 63.1 all-gather.1
where the time goes:
time: 101 us; the launch traced here: 100 us
  blocking collectives  66.7 us (66%)
  matrix products  14.5 us (14%)
  between operations  13.5 us (13%)
  local copies, waits for them, and re-layouts  2.82 us (3%)
  other arithmetic  2.2 us (2%)
    all_to_all x1, blocking collectives, per_device(): lax.all_to_all(outgoing, ('pool', 'dev'), split_axis=1, concat_axis=1, ti...  37.5 us
    all_to_all x1, blocking collectives, per_device(): lax.all_to_all(send_partial_value, ('pool', 'dev'), split_axis=1, concat_...  29.2 us
    dot_general x1, matrix products, per_device(): jnp.dot(hidden, w_down, preferred_element_type=jnp.float32)  5.49 us
    dot_general x1, matrix products, per_device(): jnp.einsum('mrd,ed->mre', tokens, lax.all_gather(router, ('pool', 'dev'),...  3.29 us
    dot_general x1, matrix products, per_device(): gate_proj = jnp.dot(flat_rows, w_gate, preferred_element_type=jnp.float32)  2.76 us
    dot_general x1, matrix products, per_device(): jnp.einsum('mrec,mecd->mrd', mixing, expert_out, precision=lax.Precision....  2.68 us
  transfers between devices with their start and end apart: 1, of which 0 were waited for; matrix products, arithmetic and copies ran while one was open for 13% of the time, Pallas kernels for 0%

commit v1 on v0

--- a/solution.py
+++ b/solution.py
@@ -1,16 +1,391 @@
+import functools
+
 import jax
 import jax.numpy as jnp
 from jax import lax
+from jax.experimental import pallas as pl
+from jax.experimental.pallas import tpu as pltpu
 from jax.sharding import PartitionSpec as P
 
 FF = 2048
 CAP = 2
-
+LINE = 4
+PAIR = 2
 
 route_scale = 2.5
-
-
-def per_device(tokens, routes, router, w_gate, w_up, w_down):
+MESH = pl.DeviceIdType.MESH
+F32 = jnp.float32
+BF16 = jnp.bfloat16
+
+
+def dot(a, b):
+    return jnp.dot(a, b, preferred_element_type=F32)
+
+
+def dot_tn(a, b):
+    return lax.dot_general(a, b, (((0,), (0,)), ((), ())), preferred_element_type=F32)
+
+
+def dot_nt(a, b):
+    return lax.dot_general(a, b, (((1,), (1,)), ((), ())), preferred_element_type=F32)
+
+
+def kernel(
+    tokens, routes, router, w_gate, w_up, w_down, out,
+    gate_v, up_v, down_v, router_v, mine, theirs, rows, parts, from_x, from_up, from_down, sums,
+    total_v, total_peer, logit_out, logit_in, logit_peer,
+    load_sem, peer_send, peer_recv, row_recv, row_up, row_down, row_x,
+    log_send, log_recv, x_send, x_recv, up_send, up_recv, down_send, down_recv,
+):
+    pool, dev = lax.axis_index("pool"), lax.axis_index("dev")
+    chips = LINE * PAIR
+    line, pair = dev // PAIR, dev % PAIR
+    n_rows, width = tokens.shape
+    half = width // 2
+    block = n_rows // 2
+    router_rows = router.shape[0]
+
+    loads = [
+        pltpu.make_async_copy(w_gate, gate_v, load_sem.at[0]),
+        pltpu.make_async_copy(w_up, up_v, load_sem.at[1]),
+        pltpu.make_async_copy(w_down, down_v, load_sem.at[2]),
+    ]
+    for load in loads:
+        load.start()
+
+    barrier = pltpu.get_barrier_semaphore()
+    pl.semaphore_signal(barrier, inc=1, device_id={"pool": 1 - pool}, device_id_type=MESH)
+    for step in range(1, chips):
+        pl.semaphore_signal(
+            barrier, inc=1, device_id={"dev": lax.rem(dev + step, chips)}, device_id_type=MESH
+        )
+
+    ids = routes[...]
+    row_no = lax.broadcasted_iota(jnp.int32, (n_rows, 8), 0)
+    slot_no = lax.broadcasted_iota(jnp.int32, (n_rows, 8), 1)
+    place = (row_no // block == (slot_no % 4) // 2) & (slot_no // 4 == pool)
+    r0 = lax.broadcasted_iota(jnp.int32, (n_rows, n_rows), 0)
+    r1 = lax.broadcasted_iota(jnp.int32, (n_rows, n_rows), 1)
+    earlier = ((r1 < r0) & (r0 // block == r1 // block)).astype(F32).astype(BF16)
+
+    def select(expert):
+        named = jnp.max((ids == expert).astype(F32), axis=1, keepdims=True)
+        named = jnp.broadcast_to(named, (n_rows, 8))
+        count = dot(earlier, named.astype(BF16))
+        hit = (named > 0.5) & place & (count == (slot_no % 2).astype(F32))
+        return hit.astype(F32)
+
+    def in_slots(sel):
+        sel = sel.astype(BF16)
+        left = dot_tn(sel, tokens[:, :half])
+        right = dot_tn(sel, tokens[:, half:])
+        return jnp.concatenate([left, right], axis=0).astype(BF16)
+
+    sel_own, sel_other = select(pool), select(1 - pool)
+    mine[...] = in_slots(sel_other)
+    router_v[pool] = router[...]
+
+    pl.semaphore_wait(barrier, chips)
+
+    def to_peer(src, dst, k):
+        return pltpu.make_async_remote_copy(
+            src, dst, peer_send.at[k], peer_recv.at[k],
+            device_id={"pool": 1 - pool}, device_id_type=MESH,
+        )
+
+    peer_rows = to_peer(mine, theirs, 0)
+    peer_rows.start()
+    peer_router = to_peer(router_v.at[pool], router_v.at[pool], 1)
+    peer_router.start()
+    own = in_slots(sel_own)
+    peer_rows.wait_recv()
+    rows[dev] = own + theirs[...]
+
+    def row_copy(z, target, sems):
+        c = z * PAIR + pair
+        return pltpu.make_async_remote_copy(
+            rows.at[c], rows.at[c], sems.at[z], row_recv.at[c],
+            device_id={"dev": target}, device_id_type=MESH,
+        )
+
+    def row_wait(c):
+        pltpu.make_async_copy(rows.at[c], rows.at[c], row_recv.at[c]).wait()
+
+    across = line * PAIR + 1 - pair
+
+    @pl.when(line < LINE - 1)
+    def _():
+        row_copy(line, dev + PAIR, row_up).start()
+
+    @pl.when(line > 0)
+    def _():
+        row_copy(line, dev - PAIR, row_down).start()
+
+    row_copy(line, across, row_x).start()
+    for d in range(1, LINE):
+        @pl.when(line - d >= 0)
+        def _():
+            z = line - d
+            row_wait(z * PAIR + pair)
+
+            @pl.when(line < LINE - 1)
+            def _():
+                row_copy(z, dev + PAIR, row_up).start()
+
+            row_copy(z, across, row_x).start()
+
+        @pl.when(line + d < LINE)
+        def _():
+            z = line + d
+            row_wait(z * PAIR + pair)
+
+            @pl.when(line > 0)
+            def _():
+                row_copy(z, dev - PAIR, row_down).start()
+
+            row_copy(z, across, row_x).start()
+
+    for z in range(LINE):
+        row_wait(z * PAIR + 1 - pair)
+    peer_router.wait_recv()
+    for load in loads:
+        load.wait()
+
+    tile = half // 4
+    hid = gate_v.shape[1]
+
+    def project(side):
+        def body(k, carry):
+            g, u, l = carry
+            at = pl.multiple_of(k * tile, 128)
+            deep = pl.multiple_of(side * half + k * tile, 128)
+            a = rows[:, :, pl.ds(at, tile)].reshape(chips * 16, tile)
+            r = router_v[:, :, pl.ds(deep, tile)].reshape(2 * router_rows, tile)
+            g = g + dot(a, gate_v[pl.ds(deep, tile), :])
+            u = u + dot(a, up_v[pl.ds(deep, tile), :])
+            l = l + dot_nt(a, r)
+            return g, u, l
+
+        zero = jnp.zeros((chips * 16, hid), F32)
+        got = lax.fori_loop(
+            0, 4, body, (zero, zero, jnp.zeros((chips * 16, 2 * router_rows), F32))
+        )
+        return [v.reshape(chips, 16, v.shape[1])[:, side * 8 : side * 8 + 8] for v in got]
+
+    (gl, ul, ll), (gr, ur, lr) = project(0), project(1)
+    gate, up = gl + gr, ul + ur
+    hidden = (gate / (1.0 + jnp.exp(-gate)) * up).astype(F32).reshape(chips * 8, hid).astype(BF16)
+    logit_out[:, :, 0 : 2 * router_rows] = ll + lr
+    logit_out[:, :, 2 * router_rows :] = jnp.zeros((chips, 8, 128 - 2 * router_rows), F32)
+    logit_in[dev] = logit_out[dev]
+
+    def log_copy(step):
+        to = lax.rem(dev + step, chips)
+        return pltpu.make_async_remote_copy(
+            logit_out.at[to], logit_in.at[dev], log_send.at[step], log_recv.at[dev],
+            device_id={"dev": to}, device_id_type=MESH,
+        )
+
+    for step in range(1, chips):
+        log_copy(step).start()
+
+    def down(t, _):
+        at = pl.multiple_of(t * tile, 128)
+        left = dot(hidden, down_v[:, pl.ds(at, tile)]).reshape(chips, 8, tile)
+        right = dot(hidden, down_v[:, pl.ds(pl.multiple_of(half + at, 128), tile)]).reshape(chips, 8, tile)
+        parts[:, :, pl.ds(at, tile)] = jnp.concatenate([left, right], axis=1).astype(BF16)
+        return 0
+
+    lax.fori_loop(0, 4, down, 0)
+
+    def x_copy(z):
+        return pltpu.make_async_remote_copy(
+            parts.at[z * PAIR + 1 - pair], from_x.at[z], x_send.at[z], x_recv.at[z],
+            device_id={"dev": across}, device_id_type=MESH,
+        )
+
+    def up_copy(z):
+        return pltpu.make_async_remote_copy(
+            sums.at[z], from_up.at[z], up_send.at[z], up_recv.at[z],
+            device_id={"dev": dev + PAIR}, device_id_type=MESH,
+        )
+
+    def down_copy(z):
+        return pltpu.make_async_remote_copy(
+            sums.at[z], from_down.at[z], down_send.at[z], down_recv.at[z],
+            device_id={"dev": dev - PAIR}, device_id_type=MESH,
+        )
+
+    def each_far_first(act_up, act_down):
+        for d in range(LINE - 1, 0, -1):
+            @pl.when(line + d < LINE)
+            def _():
+                act_up(line + d)
+
+            @pl.when(line - d >= 0)
+            def _():
+                act_down(line - d)
+
+    each_far_first(lambda z: x_copy(z).start(), lambda z: x_copy(z).start())
+    x_copy(line).start()
+
+    def paired(z):
+        x_copy(z).wait_recv()
+        return parts[z * PAIR + pair].astype(F32) + from_x[z].astype(F32)
+
+    def go_up(z):
+        total = paired(z)
+        sums[z] = total.astype(BF16)
+
+        @pl.when(line > 0)
+        def _():
+            up_copy(z).wait_recv()
+            sums[z] = (total + from_up[z].astype(F32)).astype(BF16)
+
+        up_copy(z).start()
+
+    def go_down(z):
+        total = paired(z)
+        sums[z] = total.astype(BF16)
+
+        @pl.when(line < LINE - 1)
+        def _():
+            down_copy(z).wait_recv()
+            sums[z] = (total + from_down[z].astype(F32)).astype(BF16)
+
+        down_copy(z).start()
+
+    each_far_first(go_up, go_down)
+    total_v[...] = paired(line)
+
+    for step in range(1, chips):
+        c = lax.rem(dev + step, chips)
+        pltpu.make_async_copy(logit_in.at[c], logit_in.at[c], log_recv.at[c]).wait()
+    peer_logits = to_peer(logit_in, logit_peer, 2)
+    peer_logits.start()
+
+    @pl.when(line > 0)
+    def _():
+        up_copy(line).wait_recv()
+        total_v[...] += from_up[line].astype(F32)
+
+    @pl.when(line < LINE - 1)
+    def _():
+        down_copy(line).wait_recv()
+        total_v[...] += from_down[line].astype(F32)
+
+    peer_total = to_peer(total_v, total_peer, 3)
+    peer_total.start()
+
+    lane = lax.broadcasted_iota(jnp.int32, (8, 128), 1)
+    id_bf16 = ids.astype(F32).astype(BF16)
+
+    def weigh(sel, logits, expert):
+        named = dot_tn(sel.astype(BF16), id_bf16)
+        near = jnp.zeros((8, 128), F32)
+        every = jnp.zeros((8, 128), F32)
+        for s in range(chips):
+            number = (lane // router_rows) * (chips * router_rows) + s * router_rows + lane % router_rows
+            number = jnp.where(lane < 2 * router_rows, number, -1)
+            score = 1.0 / (1.0 + jnp.exp(-logits[s]))
+            near += jnp.where(number == expert, score, 0.0)
+            match = number.astype(F32) == named[:, 0:1]
+            for k in range(1, ids.shape[1]):
+                match |= number.astype(F32) == named[:, k : k + 1]
+            every += jnp.where(match, score, 0.0)
+        near = jnp.sum(near, axis=1, keepdims=True)
+        every = jnp.sum(every, axis=1, keepdims=True)
+        return route_scale * near / every
+
+    def split(total, weight):
+        j = lax.broadcasted_iota(jnp.int32, (8, 1), 0)
+        both = []
+        for side in range(2):
+            v = jnp.where(j // 4 == pool, total[side * 8 : side * 8 + 8] * weight, 0.0)
+            hi = v.astype(BF16).astype(F32)
+            both.append(jnp.concatenate([hi, v - hi], axis=0).astype(BF16))
+        return both
+
+    own_weight = weigh(sel_own, logit_in, pool)
+    own_left, own_right = split(total_v[...], own_weight)
+    peer_logits.wait_recv()
+    other_weight = weigh(sel_other, logit_peer, 1 - pool)
+    peer_total.wait_recv()
+    other_left, other_right = split(total_peer[...], other_weight)
+    so, st = sel_own.astype(BF16), sel_other.astype(BF16)
+    mixing = jnp.concatenate([so, so, st, st], axis=1)
+    out[:, :half] = dot(mixing, jnp.concatenate([own_left, other_left], axis=0)).astype(BF16)
+    out[:, half:] = dot(mixing, jnp.concatenate([own_right, other_right], axis=0)).astype(BF16)
+
+    for copy in (peer_rows, peer_router, peer_logits, peer_total):
+        copy.wait_send()
+    for z in range(LINE):
+        row_copy(z, across, row_x).wait_send()
+        x_copy(z).wait_send()
+
+        @pl.when((line < LINE - 1) & (z <= line))
+        def _():
+            row_copy(z, dev + PAIR, row_up).wait_send()
+
+        @pl.when((line > 0) & (z >= line))
+        def _():
+            row_copy(z, dev - PAIR, row_down).wait_send()
+
+        @pl.when(z > line)
+        def _():
+            up_copy(z).wait_send()
+
+        @pl.when(z < line)
+        def _():
+            down_copy(z).wait_send()
+
+    for step in range(1, chips):
+        log_copy(step).wait_send()
+
+
+def fused(tokens, routes, router, w_gate, w_up, w_down):
+    batches, block, width = tokens.shape
+    half = width // 2
+    chips = LINE * PAIR
+    n_rows = batches * block
+    vmem = pl.BlockSpec(memory_space=pltpu.VMEM)
+    hbm = pl.BlockSpec(memory_space=pl.ANY)
+    dma = pltpu.SemaphoreType.DMA
+    out = pl.pallas_call(
+        kernel,
+        out_shape=jax.ShapeDtypeStruct((n_rows, width), BF16),
+        in_specs=[vmem, vmem, vmem, hbm, hbm, hbm],
+        out_specs=vmem,
+        scratch_shapes=[
+            pltpu.VMEM(w_gate.shape, BF16),
+            pltpu.VMEM(w_up.shape, BF16),
+            pltpu.VMEM(w_down.shape, BF16),
+            pltpu.VMEM((2, router.shape[0], width), BF16),
+            pltpu.VMEM((16, half), BF16),
+            pltpu.VMEM((16, half), BF16),
+            pltpu.VMEM((chips, 16, half), BF16),
+            pltpu.VMEM((chips, 16, half), BF16),
+            pltpu.VMEM((LINE, 16, half), BF16),
+            pltpu.VMEM((LINE, 16, half), BF16),
+            pltpu.VMEM((LINE, 16, half), BF16),
+            pltpu.VMEM((LINE, 16, half), BF16),
+            pltpu.VMEM((16, half), F32),
+            pltpu.VMEM((16, half), F32),
+            pltpu.VMEM((chips, 8, 128), F32),
+            pltpu.VMEM((chips, 8, 128), F32),
+            pltpu.VMEM((chips, 8, 128), F32),
+            dma((3,)), dma((4,)), dma((4,)), dma((chips,)), dma((LINE,)), dma((LINE,)), dma((LINE,)),
+            dma((chips,)), dma((chips,)), dma((LINE,)), dma((LINE,)), dma((LINE,)), dma((LINE,)),
+            dma((LINE,)), dma((LINE,)),
+        ],
+        compiler_params=pltpu.CompilerParams(
+            collective_id=0, has_side_effects=True, vmem_limit_bytes=44 << 20
+        ),
+    )(tokens.reshape(n_rows, width), routes.reshape(n_rows, -1), router, w_gate, w_up, w_down)
+    return out.reshape(tokens.shape)
+
+
+def spread(tokens, routes, router, w_gate, w_up, w_down):
     groups = lax.axis_size(("pool", "dev"))
     batches = tokens.shape[0]
     model_width = tokens.shape[2]
@@ -60,6 +435,8 @@
 
 
 def solution(mesh):
+    shape = dict(mesh.shape)
+    per_device = fused if (shape["pool"], shape["dev"]) == (2, LINE * PAIR) else spread
     placed = (
         P(None, ("group", "pool", "dev"), None),
         P(None, ("group", "pool", "dev"), None),

time: 101 us -> 55.3 us (0.55)
  blocking collectives: 66.7 us -> 0 us
  Pallas kernels: 0 us -> 47.1 us
  matrix products: 14.5 us -> 0 us
  between operations: 13.5 us -> 0.02 us
  local copies, waits for them, and re-layouts: 2.82 us -> 7.89 us
  other arithmetic: 2.2 us -> 0 us
    all_to_all x2 -> x0, blocking collectives: 66.7 us -> none  [the longest x1 37.5 us: per_device(): lax.all_to_all(outgoing, ('pool', 'dev'), split_axis=1, concat_axis=1, ti...]
    pallas_call x0 -> x1, Pallas kernels: none -> 47.1 us  [fused(): pl.pallas_call(kernel, out_shape=jax.ShapeDtypeStruct((n_rows, width), BF...]
    dot_general x5 -> x0, matrix products: 14.5 us -> none  [the longest x1 5.49 us: per_device(): jnp.dot(hidden, w_down, preferred_element_type=jnp.float32)]
    unnamed x4 -> x10, local copies, waits for them, and re-layouts: 0.01 us -> 7.89 us
    reshape x3 -> x0, local copies, waits for them, and re-layouts: 1.32 us -> none  [the longest x2 0.98 us: per_device(): send_partial_value = partial_value.reshape(arrived.shape)]
    reduce_sum x3 -> x0, other arithmetic: 1.11 us -> none  [the longest x1 0.8 us: per_device(): expert_out = jnp.sum(returned, axis=2, dtype=jnp.float32)]
  transfers between devices with their start and end apart: 1 -> 0, of which waited for: 0 -> 0; matrix products, arithmetic and copies ran while one was open for 13% -> 0% of each run, Pallas kernels for 0% -> 0%
where the time goes in v1:
time: 55.3 us; the launch traced here: 55 us
  Pallas kernels  47.1 us (85%)
  local copies, waits for them, and re-layouts  7.89 us (14%)
    pallas_call x1, Pallas kernels, fused(): pl.pallas_call(kernel, out_shape=jax.ShapeDtypeStruct((n_rows, width), BF...  47.1 us
    unnamed x10, local copies, waits for them, and re-layouts  7.89 us

profile of v1, /device:TPU:1, one launch (start us, length us, event | category | flops | bytes accessed | tf_op | source)
XLA Modules:
  0.0 55.0 jit_solution(6674783550273242650)
XLA Ops:
  0.0 0.8 %copy.7 = s32[2,32,8]{2,1,0:T(8,128)S(1)} copy(s32[2,32,8]{1,2,0:T(8,128)} %param.7) | data formatting | bytes 4096 | tf_op args[1]
  0.8 0.0 copy-start
  0.8 2.0 %copy-done = bf16[7168,256]{1,0:T(8,128)(2,1)S(1)} copy-done((bf16[7168,256]{1,0:T(8,128)(2,1)S(1)}, bf16[7168,256]{1,0:T(8,128)(2,1)}, u32[]{:S(2)}) %copy-start) | copy-done | bytes 3670040
  2.8 0.0 copy-start.1
  2.8 2.0 %copy-done.1 = bf16[7168,256]{1,0:T(8,128)(2,1)S(1)} copy-done((bf16[7168,256]{1,0:T(8,128)(2,1)S(1)}, bf16[7168,256]{1,0:T(8,128)(2,1)}, u32[]{:S(2)}) %copy-start.1) | copy-done | bytes 3670040
  4.9 0.0 copy-start.2
  4.9 1.2 %copy-done.2 = bf16[2,32,7168]{2,1,0:T(8,128)(2,1)S(1)} copy-done((bf16[2,32,7168]{2,1,0:T(8,128)(2,1)S(1)}, bf16[2,32,7168]{2,1,0:T(8,128)(2,1)}, u32[]{:S(2)}) %copy-start.2) | copy-done | bytes 917528
  6.0 0.0 copy-start.3
  6.0 0.9 %copy-done.3 = bf16[16,7168]{1,0:T(8,128)(2,1)S(1)} copy-done((bf16[16,7168]{1,0:T(8,128)(2,1)S(1)}, bf16[16,7168]{1,0:T(8,128)(2,1)}, u32[]{:S(2)}) %copy-start.3) | copy-done | bytes 229400
  7.0 47.1 %shard_map.64 = bf16[64,7168]{1,0:T(8,128)(2,1)S(1)} custom-call(bf16[64,7168]{1,0:T(8,128)(2,1)S(1)} %bitcast.4, s32[64,8]{1,0:T(8,128)S(1)} %bitcast.5, bf16[16,7168]{1,0:T(8,128)(2,1)S(1)} %copy-done.3, bf16[7168,256]{1,0:T(8,128)(2,1)S(1)} %copy-done, bf16[7168,256]{1,0:T(8,128)(2,1)S(1)} %copy-done.1, bf16[256,7168]{1,0:T(8,128)(2,1)} %w_down.1), custom_call_target="tpu_custom_call" | custom-call | tf_op jit(solution)/shard_map/pallas_call | solution.py:354
  54.1 0.9 %copy.9 = bf16[2,32,7168]{2,1,0:T(8,128)(2,1)} copy(bf16[2,32,7168]{2,1,0:T(8,128)(2,1)S(1)} %bitcast.3) | data formatting | bytes 1835008
Async XLA Ops:
  0.8 2.0 %copy-start = (bf16[7168,256]{1,0:T(8,128)(2,1)S(1)}, bf16[7168,256]{1,0:T(8,128)(2,1)}, u32[]{:S(2)}) copy-start(bf16[7168,256]{1,0:T(8,128)(2,1)} %w_gate.1) | copy-start | bytes 11010052
  2.8 2.0 %copy-start.1 = (bf16[7168,256]{1,0:T(8,128)(2,1)S(1)}, bf16[7168,256]{1,0:T(8,128)(2,1)}, u32[]{:S(2)}) copy-start(bf16[7168,256]{1,0:T(8,128)(2,1)} %w_up.1) | copy-start | bytes 11010052
  4.9 1.2 %copy-start.2 = (bf16[2,32,7168]{2,1,0:T(8,128)(2,1)S(1)}, bf16[2,32,7168]{2,1,0:T(8,128)(2,1)}, u32[]{:S(2)}) copy-start(bf16[2,32,7168]{2,1,0:T(8,128)(2,1)} %param.6) | copy-start | bytes 2752516
  6.0 0.9 %copy-start.3 = (bf16[16,7168]{1,0:T(8,128)(2,1)S(1)}, bf16[16,7168]{1,0:T(8,128)(2,1)}, u32[]{:S(2)}) copy-start(bf16[16,7168]{1,0:T(8,128)(2,1)} %router.1) | copy-start | bytes 688132

commit v2 on v1

--- a/solution.py
+++ b/solution.py
@@ -31,8 +31,8 @@
 
 
 def kernel(
-    tokens, routes, router, w_gate, w_up, w_down, out,
-    gate_v, up_v, down_v, router_v, mine, theirs, rows, parts, from_x, from_up, from_down, sums,
+    tokens_hbm, routes, router, w_gate, w_up, w_down, out,
+    tokens, gate_v, up_v, down_v, router_v, mine, theirs, rows, parts, from_x, from_up, from_down, sums,
     total_v, total_peer, logit_out, logit_in, logit_peer,
     load_sem, peer_send, peer_recv, row_recv, row_up, row_down, row_x,
     log_send, log_recv, x_send, x_recv, up_send, up_recv, down_send, down_recv,
@@ -45,14 +45,15 @@
     block = n_rows // 2
     router_rows = router.shape[0]
 
+    own_router = pltpu.make_async_copy(router, router_v.at[pool], load_sem.at[3])
+    own_router.start()
+    own_tokens = pltpu.make_async_copy(tokens_hbm, tokens, load_sem.at[4])
+    own_tokens.start()
     loads = [
         pltpu.make_async_copy(w_gate, gate_v, load_sem.at[0]),
         pltpu.make_async_copy(w_up, up_v, load_sem.at[1]),
         pltpu.make_async_copy(w_down, down_v, load_sem.at[2]),
     ]
-    for load in loads:
-        load.start()
-
     barrier = pltpu.get_barrier_semaphore()
     pl.semaphore_signal(barrier, inc=1, device_id={"pool": 1 - pool}, device_id_type=MESH)
     for step in range(1, chips):
@@ -60,30 +61,33 @@
             barrier, inc=1, device_id={"dev": lax.rem(dev + step, chips)}, device_id_type=MESH
         )
 
-    ids = routes[...]
-    row_no = lax.broadcasted_iota(jnp.int32, (n_rows, 8), 0)
-    slot_no = lax.broadcasted_iota(jnp.int32, (n_rows, 8), 1)
+    ids = jnp.concatenate([routes[0], routes[1]], axis=1)
+    slot_no = lax.broadcasted_iota(jnp.int32, (8, n_rows), 0)
+    row_no = lax.broadcasted_iota(jnp.int32, (8, n_rows), 1)
     place = (row_no // block == (slot_no % 4) // 2) & (slot_no // 4 == pool)
     r0 = lax.broadcasted_iota(jnp.int32, (n_rows, n_rows), 0)
     r1 = lax.broadcasted_iota(jnp.int32, (n_rows, n_rows), 1)
-    earlier = ((r1 < r0) & (r0 // block == r1 // block)).astype(F32).astype(BF16)
+    earlier = ((r0 < r1) & (r0 // block == r1 // block)).astype(F32).astype(BF16)
 
     def select(expert):
-        named = jnp.max((ids == expert).astype(F32), axis=1, keepdims=True)
-        named = jnp.broadcast_to(named, (n_rows, 8))
-        count = dot(earlier, named.astype(BF16))
+        named = jnp.max((ids == expert).astype(F32), axis=0, keepdims=True)
+        named = jnp.broadcast_to(named, (8, n_rows))
+        count = dot(named.astype(BF16), earlier)
         hit = (named > 0.5) & place & (count == (slot_no % 2).astype(F32))
         return hit.astype(F32)
 
     def in_slots(sel):
         sel = sel.astype(BF16)
-        left = dot_tn(sel, tokens[:, :half])
-        right = dot_tn(sel, tokens[:, half:])
+        left = dot(sel, tokens[:, :half])
+        right = dot(sel, tokens[:, half:])
         return jnp.concatenate([left, right], axis=0).astype(BF16)
 
     sel_own, sel_other = select(pool), select(1 - pool)
+    own_tokens.wait()
+    own_router.wait()
+    for load in loads:
+        load.start()
     mine[...] = in_slots(sel_other)
-    router_v[pool] = router[...]
 
     pl.semaphore_wait(barrier, chips)
 
@@ -281,7 +285,7 @@
     id_bf16 = ids.astype(F32).astype(BF16)
 
     def weigh(sel, logits, expert):
-        named = dot_tn(sel.astype(BF16), id_bf16)
+        named = dot_nt(sel.astype(BF16), id_bf16)
         near = jnp.zeros((8, 128), F32)
         every = jnp.zeros((8, 128), F32)
         for s in range(chips):
@@ -290,7 +294,7 @@
             score = 1.0 / (1.0 + jnp.exp(-logits[s]))
             near += jnp.where(number == expert, score, 0.0)
             match = number.astype(F32) == named[:, 0:1]
-            for k in range(1, ids.shape[1]):
+            for k in range(1, ids.shape[0]):
                 match |= number.astype(F32) == named[:, k : k + 1]
             every += jnp.where(match, score, 0.0)
         near = jnp.sum(near, axis=1, keepdims=True)
@@ -312,10 +316,9 @@
     other_weight = weigh(sel_other, logit_peer, 1 - pool)
     peer_total.wait_recv()
     other_left, other_right = split(total_peer[...], other_weight)
-    so, st = sel_own.astype(BF16), sel_other.astype(BF16)
-    mixing = jnp.concatenate([so, so, st, st], axis=1)
-    out[:, :half] = dot(mixing, jnp.concatenate([own_left, other_left], axis=0)).astype(BF16)
-    out[:, half:] = dot(mixing, jnp.concatenate([own_right, other_right], axis=0)).astype(BF16)
+    mixing = jnp.concatenate([sel_own, sel_own, sel_other, sel_other], axis=0).astype(BF16)
+    out[:, :half] = dot_tn(mixing, jnp.concatenate([own_left, other_left], axis=0)).astype(BF16)
+    out[:, half:] = dot_tn(mixing, jnp.concatenate([own_right, other_right], axis=0)).astype(BF16)
 
     for copy in (peer_rows, peer_router, peer_logits, peer_total):
         copy.wait_send()
@@ -349,14 +352,15 @@
     chips = LINE * PAIR
     n_rows = batches * block
     vmem = pl.BlockSpec(memory_space=pltpu.VMEM)
-    hbm = pl.BlockSpec(memory_space=pl.ANY)
+    hbm = pl.BlockSpec(memory_space=pltpu.HBM)
     dma = pltpu.SemaphoreType.DMA
     out = pl.pallas_call(
         kernel,
         out_shape=jax.ShapeDtypeStruct((n_rows, width), BF16),
-        in_specs=[vmem, vmem, vmem, hbm, hbm, hbm],
+        in_specs=[hbm, vmem, hbm, hbm, hbm, hbm],
         out_specs=vmem,
         scratch_shapes=[
+            pltpu.VMEM((n_rows, width), BF16),
             pltpu.VMEM(w_gate.shape, BF16),
             pltpu.VMEM(w_up.shape, BF16),
             pltpu.VMEM(w_down.shape, BF16),
@@ -374,14 +378,14 @@
             pltpu.VMEM((chips, 8, 128), F32),
             pltpu.VMEM((chips, 8, 128), F32),
             pltpu.VMEM((chips, 8, 128), F32),
-            dma((3,)), dma((4,)), dma((4,)), dma((chips,)), dma((LINE,)), dma((LINE,)), dma((LINE,)),
+            dma((5,)), dma((4,)), dma((4,)), dma((chips,)), dma((LINE,)), dma((LINE,)), dma((LINE,)),
             dma((chips,)), dma((chips,)), dma((LINE,)), dma((LINE,)), dma((LINE,)), dma((LINE,)),
             dma((LINE,)), dma((LINE,)),
         ],
         compiler_params=pltpu.CompilerParams(
-            collective_id=0, has_side_effects=True, vmem_limit_bytes=44 << 20
+            collective_id=0, has_side_effects=True, vmem_limit_bytes=(64 << 20) - (256 << 10)
         ),
-    )(tokens.reshape(n_rows, width), routes.reshape(n_rows, -1), router, w_gate, w_up, w_down)
+    )(tokens.reshape(n_rows, width), routes.transpose(0, 2, 1), router, w_gate, w_up, w_down)
     return out.reshape(tokens.shape)
 
 

time: 55.3 us -> 50.6 us (0.915)
  local copies, waits for them, and re-layouts: 7.89 us -> 2.16 us
  Pallas kernels: 47.1 us -> 48.2 us
    unnamed x10 -> x1, local copies, waits for them, and re-layouts: 7.89 us -> 2.16 us
    pallas_call x1, Pallas kernels: 47.1 us -> 48.2 us  [fused(): pl.pallas_call(kernel, out_shape=jax.ShapeDtypeStruct((n_rows, width), BF...]
where the time goes in v2:
time: 50.6 us; the launch traced here: 50.4 us
  Pallas kernels  48.2 us (95%)
  local copies, waits for them, and re-layouts  2.16 us (4%)
    pallas_call x1, Pallas kernels, fused(): pl.pallas_call(kernel, out_shape=jax.ShapeDtypeStruct((n_rows, width), BF...  48.2 us
    unnamed x1, local copies, waits for them, and re-layouts  2.16 us

profile of v2, /device:TPU:1, one launch (start us, length us, event | category | flops | bytes accessed | tf_op | source)
XLA Modules:
  0.0 50.4 jit_solution(4723659091112480344)
XLA Ops:
  0.0 48.2 %shard_map.64 = bf16[64,7168]{1,0:T(8,128)(2,1)} custom-call(bf16[64,7168]{1,0:T(8,128)(2,1)} %bitcast.4, s32[2,8,32]{2,1,0:T(8,128)} %bitcast.5, bf16[16,7168]{1,0:T(8,128)(2,1)} %router.1, bf16[7168,256]{1,0:T(8,128)(2,1)} %w_gate.1, bf16[7168,256]{1,0:T(8,128)(2,1)} %w_up.1, bf16[256,7168]{1,0:T(8,128)(2,1)} %w_down.1), custom_call_target="tpu_custom_call" | custom-call | tf_op jit(solution)/shard_map/pallas_call | solution.py:357
  48.2 2.2 %copy.8 = bf16[2,32,7168]{2,1,0:T(8,128)(2,1)} copy(bf16[2,32,7168]{2,1,0:T(8,128)(2,1)} %bitcast.3) | data formatting | bytes 1835008

commit v3 on v2

--- a/solution.py
+++ b/solution.py
@@ -11,6 +11,7 @@
 CAP = 2
 LINE = 4
 PAIR = 2
+PIECES = 2
 
 route_scale = 2.5
 MESH = pl.DeviceIdType.MESH
@@ -31,7 +32,7 @@
 
 
 def kernel(
-    tokens_hbm, routes, router, w_gate, w_up, w_down, out,
+    tokens_hbm, routes, router, w_gate, w_up, w_down, values, mixing,
     tokens, gate_v, up_v, down_v, router_v, mine, theirs, rows, parts, from_x, from_up, from_down, sums,
     total_v, total_peer, logit_out, logit_in, logit_peer,
     load_sem, peer_send, peer_recv, row_recv, row_up, row_down, row_x,
@@ -42,6 +43,7 @@
     line, pair = dev // PAIR, dev % PAIR
     n_rows, width = tokens.shape
     half = width // 2
+    piece = half // PIECES
     block = n_rows // 2
     router_rows = router.shape[0]
 
@@ -76,10 +78,10 @@
         hit = (named > 0.5) & place & (count == (slot_no % 2).astype(F32))
         return hit.astype(F32)
 
-    def in_slots(sel):
+    def in_slots(sel, p):
         sel = sel.astype(BF16)
-        left = dot(sel, tokens[:, :half])
-        right = dot(sel, tokens[:, half:])
+        left = dot(sel, tokens[:, p * piece : (p + 1) * piece])
+        right = dot(sel, tokens[:, half + p * piece : half + (p + 1) * piece])
         return jnp.concatenate([left, right], axis=0).astype(BF16)
 
     sel_own, sel_other = select(pool), select(1 - pool)
@@ -87,7 +89,8 @@
     own_router.wait()
     for load in loads:
         load.start()
-    mine[...] = in_slots(sel_other)
+    for p in range(PIECES):
+        mine[p] = in_slots(sel_other, p)
 
     pl.semaphore_wait(barrier, chips)
 
@@ -97,82 +100,85 @@
             device_id={"pool": 1 - pool}, device_id_type=MESH,
         )
 
-    peer_rows = to_peer(mine, theirs, 0)
-    peer_rows.start()
-    peer_router = to_peer(router_v.at[pool], router_v.at[pool], 1)
+    peer_rows = [to_peer(mine.at[p], theirs.at[p], p) for p in range(PIECES)]
+    for copy in peer_rows:
+        copy.start()
+    peer_router = to_peer(router_v.at[pool], router_v.at[pool], 2 * PIECES)
     peer_router.start()
-    own = in_slots(sel_own)
-    peer_rows.wait_recv()
-    rows[dev] = own + theirs[...]
-
-    def row_copy(z, target, sems):
+
+    def row_copy(p, z, target, sems):
         c = z * PAIR + pair
         return pltpu.make_async_remote_copy(
-            rows.at[c], rows.at[c], sems.at[z], row_recv.at[c],
+            rows.at[p, c], rows.at[p, c], sems.at[p, z], row_recv.at[p, c],
             device_id={"dev": target}, device_id_type=MESH,
         )
 
-    def row_wait(c):
-        pltpu.make_async_copy(rows.at[c], rows.at[c], row_recv.at[c]).wait()
+    def row_wait(p, c):
+        pltpu.make_async_copy(rows.at[p, c], rows.at[p, c], row_recv.at[p, c]).wait()
 
     across = line * PAIR + 1 - pair
-
-    @pl.when(line < LINE - 1)
-    def _():
-        row_copy(line, dev + PAIR, row_up).start()
-
-    @pl.when(line > 0)
-    def _():
-        row_copy(line, dev - PAIR, row_down).start()
-
-    row_copy(line, across, row_x).start()
+    for p in range(PIECES):
+        own = in_slots(sel_own, p)
+        peer_rows[p].wait_recv()
+        rows[p, dev] = own + theirs[p]
+
+        @pl.when(line < LINE - 1)
+        def _():
+            row_copy(p, line, dev + PAIR, row_up).start()
+
+        @pl.when(line > 0)
+        def _():
+            row_copy(p, line, dev - PAIR, row_down).start()
+
+        row_copy(p, line, across, row_x).start()
+
     for d in range(1, LINE):
-        @pl.when(line - d >= 0)
-        def _():
-            z = line - d
-            row_wait(z * PAIR + pair)
-
-            @pl.when(line < LINE - 1)
+        for p in range(PIECES):
+            @pl.when(line - d >= 0)
             def _():
-                row_copy(z, dev + PAIR, row_up).start()
-
-            row_copy(z, across, row_x).start()
-
-        @pl.when(line + d < LINE)
-        def _():
-            z = line + d
-            row_wait(z * PAIR + pair)
-
-            @pl.when(line > 0)
+                z = line - d
+                row_wait(p, z * PAIR + pair)
+
+                @pl.when(line < LINE - 1)
+                def _():
+                    row_copy(p, z, dev + PAIR, row_up).start()
+
+                row_copy(p, z, across, row_x).start()
+
+            @pl.when(line + d < LINE)
             def _():
-                row_copy(z, dev - PAIR, row_down).start()
-
-            row_copy(z, across, row_x).start()
-
-    for z in range(LINE):
-        row_wait(z * PAIR + 1 - pair)
+                z = line + d
+                row_wait(p, z * PAIR + pair)
+
+                @pl.when(line > 0)
+                def _():
+                    row_copy(p, z, dev - PAIR, row_down).start()
+
+                row_copy(p, z, across, row_x).start()
+
     peer_router.wait_recv()
     for load in loads:
         load.wait()
-
-    tile = half // 4
+    for p in range(PIECES):
+        for z in range(LINE):
+            row_wait(p, z * PAIR + 1 - pair)
+
     hid = gate_v.shape[1]
 
     def project(side):
         def body(k, carry):
             g, u, l = carry
-            at = pl.multiple_of(k * tile, 128)
-            deep = pl.multiple_of(side * half + k * tile, 128)
-            a = rows[:, :, pl.ds(at, tile)].reshape(chips * 16, tile)
-            r = router_v[:, :, pl.ds(deep, tile)].reshape(2 * router_rows, tile)
-            g = g + dot(a, gate_v[pl.ds(deep, tile), :])
-            u = u + dot(a, up_v[pl.ds(deep, tile), :])
+            deep = pl.multiple_of(side * half + k * piece, 128)
+            a = rows[k].reshape(chips * 16, piece)
+            r = router_v[:, :, pl.ds(deep, piece)].reshape(2 * router_rows, piece)
+            g = g + dot(a, gate_v[pl.ds(deep, piece), :])
+            u = u + dot(a, up_v[pl.ds(deep, piece), :])
             l = l + dot_nt(a, r)
             return g, u, l
 
         zero = jnp.zeros((chips * 16, hid), F32)
         got = lax.fori_loop(
-            0, 4, body, (zero, zero, jnp.zeros((chips * 16, 2 * router_rows), F32))
+            0, PIECES, body, (zero, zero, jnp.zeros((chips * 16, 2 * router_rows), F32))
         )
         return [v.reshape(chips, 16, v.shape[1])[:, side * 8 : side * 8 + 8] for v in got]
 
@@ -193,30 +199,21 @@
     for step in range(1, chips):
         log_copy(step).start()
 
-    def down(t, _):
-        at = pl.multiple_of(t * tile, 128)
-        left = dot(hidden, down_v[:, pl.ds(at, tile)]).reshape(chips, 8, tile)
-        right = dot(hidden, down_v[:, pl.ds(pl.multiple_of(half + at, 128), tile)]).reshape(chips, 8, tile)
-        parts[:, :, pl.ds(at, tile)] = jnp.concatenate([left, right], axis=1).astype(BF16)
-        return 0
-
-    lax.fori_loop(0, 4, down, 0)
-
-    def x_copy(z):
-        return pltpu.make_async_remote_copy(
-            parts.at[z * PAIR + 1 - pair], from_x.at[z], x_send.at[z], x_recv.at[z],
+    def x_copy(p, z):
+        return pltpu.make_async_remote_copy(
+            parts.at[p, z * PAIR + 1 - pair], from_x.at[p, z], x_send.at[p, z], x_recv.at[p, z],
             device_id={"dev": across}, device_id_type=MESH,
         )
 
-    def up_copy(z):
-        return pltpu.make_async_remote_copy(
-            sums.at[z], from_up.at[z], up_send.at[z], up_recv.at[z],
+    def up_copy(p, z):
+        return pltpu.make_async_remote_copy(
+            sums.at[p, z], from_up.at[p, z], up_send.at[p, z], up_recv.at[p, z],
             device_id={"dev": dev + PAIR}, device_id_type=MESH,
         )
 
-    def down_copy(z):
-        return pltpu.make_async_remote_copy(
-            sums.at[z], from_down.at[z], down_send.at[z], down_recv.at[z],
+    def down_copy(p, z):
+        return pltpu.make_async_remote_copy(
+            sums.at[p, z], from_down.at[p, z], down_send.at[p, z], down_recv.at[p, z],
             device_id={"dev": dev - PAIR}, device_id_type=MESH,
         )
 
@@ -230,56 +227,13 @@
             def _():
                 act_down(line - d)
 
-    each_far_first(lambda z: x_copy(z).start(), lambda z: x_copy(z).start())
-    x_copy(line).start()
-
-    def paired(z):
-        x_copy(z).wait_recv()
-        return parts[z * PAIR + pair].astype(F32) + from_x[z].astype(F32)
-
-    def go_up(z):
-        total = paired(z)
-        sums[z] = total.astype(BF16)
-
-        @pl.when(line > 0)
-        def _():
-            up_copy(z).wait_recv()
-            sums[z] = (total + from_up[z].astype(F32)).astype(BF16)
-
-        up_copy(z).start()
-
-    def go_down(z):
-        total = paired(z)
-        sums[z] = total.astype(BF16)
-
-        @pl.when(line < LINE - 1)
-        def _():
-            down_copy(z).wait_recv()
-            sums[z] = (total + from_down[z].astype(F32)).astype(BF16)
-
-        down_copy(z).start()
-
-    each_far_first(go_up, go_down)
-    total_v[...] = paired(line)
-
-    for step in range(1, chips):
-        c = lax.rem(dev + step, chips)
-        pltpu.make_async_copy(logit_in.at[c], logit_in.at[c], log_recv.at[c]).wait()
-    peer_logits = to_peer(logit_in, logit_peer, 2)
-    peer_logits.start()
-
-    @pl.when(line > 0)
-    def _():
-        up_copy(line).wait_recv()
-        total_v[...] += from_up[line].astype(F32)
-
-    @pl.when(line < LINE - 1)
-    def _():
-        down_copy(line).wait_recv()
-        total_v[...] += from_down[line].astype(F32)
-
-    peer_total = to_peer(total_v, total_peer, 3)
-    peer_total.start()
+    for p in range(PIECES):
+        left = dot(hidden, down_v[:, p * piece : (p + 1) * piece])
+        right = dot(hidden, down_v[:, half + p * piece : half + (p + 1) * piece])
+        both = [left.reshape(chips, 8, piece), right.reshape(chips, 8, piece)]
+        parts[p] = jnp.concatenate(both, axis=1).astype(BF16)
+        each_far_first(lambda z: x_copy(p, z).start(), lambda z: x_copy(p, z).start())
+        x_copy(p, line).start()
 
     lane = lax.broadcasted_iota(jnp.int32, (8, 128), 1)
     id_bf16 = ids.astype(F32).astype(BF16)
@@ -310,37 +264,112 @@
             both.append(jnp.concatenate([hi, v - hi], axis=0).astype(BF16))
         return both
 
+    for step in range(1, chips):
+        c = lax.rem(dev + step, chips)
+        pltpu.make_async_copy(logit_in.at[c], logit_in.at[c], log_recv.at[c]).wait()
+    peer_logits = to_peer(logit_in, logit_peer, 2 * PIECES + 1)
+    peer_logits.start()
     own_weight = weigh(sel_own, logit_in, pool)
-    own_left, own_right = split(total_v[...], own_weight)
+
+    def paired(p, z):
+        x_copy(p, z).wait_recv()
+        return parts[p, z * PAIR + pair].astype(F32) + from_x[p, z].astype(F32)
+
+    def go_up(p, z):
+        total = paired(p, z)
+
+        @pl.when(line > 0)
+        def _():
+            up_copy(p, z).wait_recv()
+            sums[p, z] = (total + from_up[p, z].astype(F32)).astype(BF16)
+
+        @pl.when(line == 0)
+        def _():
+            sums[p, z] = total.astype(BF16)
+
+        up_copy(p, z).start()
+
+    def go_down(p, z):
+        total = paired(p, z)
+
+        @pl.when(line < LINE - 1)
+        def _():
+            down_copy(p, z).wait_recv()
+            sums[p, z] = (total + from_down[p, z].astype(F32)).astype(BF16)
+
+        @pl.when(line == LINE - 1)
+        def _():
+            sums[p, z] = total.astype(BF16)
+
+        down_copy(p, z).start()
+
+    peer_total = [
+        to_peer(total_v.at[p], total_peer.at[p], PIECES + p) for p in range(PIECES)
+    ]
+
+    def finish(p):
+        total_v[p] = paired(p, line)
+
+        @pl.when(line > 0)
+        def _():
+            up_copy(p, line).wait_recv()
+            total_v[p] += from_up[p, line].astype(F32)
+
+        @pl.when(line < LINE - 1)
+        def _():
+            down_copy(p, line).wait_recv()
+            total_v[p] += from_down[p, line].astype(F32)
+
+        peer_total[p].start()
+
+    for p in range(PIECES):
+        each_far_first(lambda z: go_up(p, z), lambda z: go_down(p, z))
+        if p:
+            finish(p - 1)
     peer_logits.wait_recv()
     other_weight = weigh(sel_other, logit_peer, 1 - pool)
-    peer_total.wait_recv()
-    other_left, other_right = split(total_peer[...], other_weight)
-    mixing = jnp.concatenate([sel_own, sel_own, sel_other, sel_other], axis=0).astype(BF16)
-    out[:, :half] = dot_tn(mixing, jnp.concatenate([own_left, other_left], axis=0)).astype(BF16)
-    out[:, half:] = dot_tn(mixing, jnp.concatenate([own_right, other_right], axis=0)).astype(BF16)
-
-    for copy in (peer_rows, peer_router, peer_logits, peer_total):
+
+    def mix(sel, weight):
+        return jnp.where(sel > 0.5, jnp.broadcast_to(weight * 0.0 + 1.0, sel.shape), 0.0)
+
+    own_mix, other_mix = mix(sel_own, own_weight), mix(sel_other, other_weight)
+    mixing[...] = jnp.concatenate([own_mix, own_mix, other_mix, other_mix], axis=0).astype(BF16)
+    own_weight = jnp.where(own_weight == own_weight, own_weight, 0.0)
+    other_weight = jnp.where(other_weight == other_weight, other_weight, 0.0)
+    finish(PIECES - 1)
+
+    def give(p, total, weight, first):
+        left, right = split(total, weight)
+        values[first : first + 16, p * piece : (p + 1) * piece] = left
+        values[first : first + 16, half + p * piece : half + (p + 1) * piece] = right
+
+    for p in range(PIECES):
+        give(p, total_v[p], own_weight, 0)
+    for p in range(PIECES):
+        peer_total[p].wait_recv()
+        give(p, total_peer[p], other_weight, 16)
+
+    for copy in (*peer_rows, peer_router, peer_logits, *peer_total):
         copy.wait_send()
-    for z in range(LINE):
-        row_copy(z, across, row_x).wait_send()
-        x_copy(z).wait_send()
+    for p, z in [(p, z) for p in range(PIECES) for z in range(LINE)]:
+        row_copy(p, z, across, row_x).wait_send()
+        x_copy(p, z).wait_send()
 
         @pl.when((line < LINE - 1) & (z <= line))
         def _():
-            row_copy(z, dev + PAIR, row_up).wait_send()
+            row_copy(p, z, dev + PAIR, row_up).wait_send()
 
         @pl.when((line > 0) & (z >= line))
         def _():
-            row_copy(z, dev - PAIR, row_down).wait_send()
+            row_copy(p, z, dev - PAIR, row_down).wait_send()
 
         @pl.when(z > line)
         def _():
-            up_copy(z).wait_send()
+            up_copy(p, z).wait_send()
 
         @pl.when(z < line)
         def _():
-            down_copy(z).wait_send()
+            down_copy(p, z).wait_send()
 
     for step in range(1, chips):
         log_copy(step).wait_send()
@@ -354,39 +383,40 @@
     vmem = pl.BlockSpec(memory_space=pltpu.VMEM)
     hbm = pl.BlockSpec(memory_space=pltpu.HBM)
     dma = pltpu.SemaphoreType.DMA
-    out = pl.pallas_call(
+    values, mixing = pl.pallas_call(
         kernel,
-        out_shape=jax.ShapeDtypeStruct((n_rows, width), BF16),
+        out_shape=(jax.ShapeDtypeStruct((32, width), BF16), jax.ShapeDtypeStruct((32, n_rows), BF16)),
         in_specs=[hbm, vmem, hbm, hbm, hbm, hbm],
-        out_specs=vmem,
+        out_specs=(vmem, vmem),
         scratch_shapes=[
             pltpu.VMEM((n_rows, width), BF16),
             pltpu.VMEM(w_gate.shape, BF16),
             pltpu.VMEM(w_up.shape, BF16),
             pltpu.VMEM(w_down.shape, BF16),
             pltpu.VMEM((2, router.shape[0], width), BF16),
-            pltpu.VMEM((16, half), BF16),
-            pltpu.VMEM((16, half), BF16),
-            pltpu.VMEM((chips, 16, half), BF16),
-            pltpu.VMEM((chips, 16, half), BF16),
-            pltpu.VMEM((LINE, 16, half), BF16),
-            pltpu.VMEM((LINE, 16, half), BF16),
-            pltpu.VMEM((LINE, 16, half), BF16),
-            pltpu.VMEM((LINE, 16, half), BF16),
-            pltpu.VMEM((16, half), F32),
-            pltpu.VMEM((16, half), F32),
+            pltpu.VMEM((PIECES, 16, half // PIECES), BF16),
+            pltpu.VMEM((PIECES, 16, half // PIECES), BF16),
+            pltpu.VMEM((PIECES, chips, 16, half // PIECES), BF16),
+            pltpu.VMEM((PIECES, chips, 16, half // PIECES), BF16),
+            pltpu.VMEM((PIECES, LINE, 16, half // PIECES), BF16),
+            pltpu.VMEM((PIECES, LINE, 16, half // PIECES), BF16),
+            pltpu.VMEM((PIECES, LINE, 16, half // PIECES), BF16),
+            pltpu.VMEM((PIECES, LINE, 16, half // PIECES), BF16),
+            pltpu.VMEM((PIECES, 16, half // PIECES), F32),
+            pltpu.VMEM((PIECES, 16, half // PIECES), F32),
             pltpu.VMEM((chips, 8, 128), F32),
             pltpu.VMEM((chips, 8, 128), F32),
             pltpu.VMEM((chips, 8, 128), F32),
-            dma((5,)), dma((4,)), dma((4,)), dma((chips,)), dma((LINE,)), dma((LINE,)), dma((LINE,)),
-            dma((chips,)), dma((chips,)), dma((LINE,)), dma((LINE,)), dma((LINE,)), dma((LINE,)),
-            dma((LINE,)), dma((LINE,)),
+            dma((5,)), dma((2 * PIECES + 2,)), dma((2 * PIECES + 2,)), dma((PIECES, chips)),
+            dma((PIECES, LINE)), dma((PIECES, LINE)), dma((PIECES, LINE)),
+            dma((chips,)), dma((chips,)), dma((PIECES, LINE)), dma((PIECES, LINE)),
+            dma((PIECES, LINE)), dma((PIECES, LINE)), dma((PIECES, LINE)), dma((PIECES, LINE)),
         ],
         compiler_params=pltpu.CompilerParams(
             collective_id=0, has_side_effects=True, vmem_limit_bytes=(64 << 20) - (256 << 10)
         ),
     )(tokens.reshape(n_rows, width), routes.transpose(0, 2, 1), router, w_gate, w_up, w_down)
-    return out.reshape(tokens.shape)
+    return dot_tn(mixing, values).astype(BF16).reshape(tokens.shape)
 
 
 def spread(tokens, routes, router, w_gate, w_up, w_down):

time: 50.6 us -> 48.7 us (0.962)
  matrix products: 0 us -> 2.38 us
  Pallas kernels: 48.2 us -> 46 us
  local copies, waits for them, and re-layouts: 2.16 us -> 0 us
    dot_general x0 -> x1, matrix products: none -> 2.38 us  [dot_tn(): lax.dot_general(a, b, (((0,), (0,)), ((), ())), preferred_element_type=F32)]
    pallas_call x1, Pallas kernels: 48.2 us -> 46 us  [fused(): pl.pallas_call(kernel, out_shape=(jax.ShapeDtypeStruct((32, width), BF16)...]
    unnamed x1 -> x0, local copies, waits for them, and re-layouts: 2.16 us -> none
where the time goes in v3:
time: 48.7 us; the launch traced here: 48.4 us
  Pallas kernels  46 us (94%)
  matrix products  2.38 us (5%)
    pallas_call x1, Pallas kernels, fused(): pl.pallas_call(kernel, out_shape=(jax.ShapeDtypeStruct((32, width), BF16)...  46 us
    dot_general x1, matrix products, dot_tn(): lax.dot_general(a, b, (((0,), (0,)), ((), ())), preferred_element_type=F32)  2.38 us

profile of v3, /device:TPU:1, one launch (start us, length us, event | category | flops | bytes accessed | tf_op | source)
XLA Modules:
  0.0 48.4 jit_solution(7751482421475182827)
XLA Ops:
  0.0 46.0 %shard_map.64 = (bf16[32,7168]{1,0:T(8,128)(2,1)}, bf16[32,64]{1,0:T(8,128)(2,1)}) custom-call(bf16[64,7168]{1,0:T(8,128)(2,1)} %bitcast.5, s32[2,8,32]{2,1,0:T(8,128)} %bitcast.6, bf16[16,7168]{1,0:T(8,128)(2,1)} %router.1, bf16[7168,256]{1,0:T(8,128)(2,1)} %w_gate.1, bf16[7168,256]{1,0:T(8,128)(2,1)} %w_up.1, bf16[256,7168]{1,0:T(8,128)(2,1)} %w_down.1), custom_call_target="tpu_custom_call" | custom-call | tf_op jit(solution)/shard_map/pallas_call | solution.py:386
  46.0 2.4 %convolution_convert_fusion = bf16[64,7168]{1,0:T(8,128)(2,1)} fusion(bf16[32,64]{1,0:T(8,128)(2,1)} %get-tuple-element.7, bf16[32,7168]{1,0:T(8,128)(2,1)} %get-tuple-element.8), kind=kOutput, calls=%fused_computation | convolution fusion | flops 29818880 | bytes 1380352 | tf_op jit(solution)/shard_map/dot_general | solution.py:27

commit v4 on v3

--- a/solution.py
+++ b/solution.py
@@ -32,8 +32,8 @@
 
 
 def kernel(
-    tokens_hbm, routes, router, w_gate, w_up, w_down, values, mixing,
-    tokens, gate_v, up_v, down_v, router_v, mine, theirs, rows, parts, from_x, from_up, from_down, sums,
+    tokens_hbm, routes, router, w_gate, w_up, w_down, out,
+    tokens, values, gate_v, up_v, down_v, router_v, mine, theirs, rows, parts, from_x, from_up, from_down, sums,
     total_v, total_peer, logit_out, logit_in, logit_peer,
     load_sem, peer_send, peer_recv, row_recv, row_up, row_down, row_x,
     log_send, log_recv, x_send, x_recv, up_send, up_recv, down_send, down_recv,
@@ -333,7 +333,7 @@
         return jnp.where(sel > 0.5, jnp.broadcast_to(weight * 0.0 + 1.0, sel.shape), 0.0)
 
     own_mix, other_mix = mix(sel_own, own_weight), mix(sel_other, other_weight)
-    mixing[...] = jnp.concatenate([own_mix, own_mix, other_mix, other_mix], axis=0).astype(BF16)
+    mixing = jnp.concatenate([own_mix, own_mix, other_mix, other_mix], axis=0).astype(BF16)
     own_weight = jnp.where(own_weight == own_weight, own_weight, 0.0)
     other_weight = jnp.where(other_weight == other_weight, other_weight, 0.0)
     finish(PIECES - 1)
@@ -348,6 +348,8 @@
     for p in range(PIECES):
         peer_total[p].wait_recv()
         give(p, total_peer[p], other_weight, 16)
+        for low in (p * piece, half + p * piece):
+            out[:, low : low + piece] = dot_tn(mixing, values[:, low : low + piece]).astype(BF16)
 
     for copy in (*peer_rows, peer_router, peer_logits, *peer_total):
         copy.wait_send()
@@ -383,13 +385,14 @@
     vmem = pl.BlockSpec(memory_space=pltpu.VMEM)
     hbm = pl.BlockSpec(memory_space=pltpu.HBM)
     dma = pltpu.SemaphoreType.DMA
-    values, mixing = pl.pallas_call(
+    out = pl.pallas_call(
         kernel,
-        out_shape=(jax.ShapeDtypeStruct((32, width), BF16), jax.ShapeDtypeStruct((32, n_rows), BF16)),
+        out_shape=jax.ShapeDtypeStruct((n_rows, width), BF16),
         in_specs=[hbm, vmem, hbm, hbm, hbm, hbm],
-        out_specs=(vmem, vmem),
+        out_specs=vmem,
         scratch_shapes=[
             pltpu.VMEM((n_rows, width), BF16),
+            pltpu.VMEM((32, width), BF16),
             pltpu.VMEM(w_gate.shape, BF16),
             pltpu.VMEM(w_up.shape, BF16),
             pltpu.VMEM(w_down.shape, BF16),
@@ -413,10 +416,10 @@
             dma((PIECES, LINE)), dma((PIECES, LINE)), dma((PIECES, LINE)), dma((PIECES, LINE)),
         ],
         compiler_params=pltpu.CompilerParams(
-            collective_id=0, has_side_effects=True, vmem_limit_bytes=(64 << 20) - (256 << 10)
+            collective_id=0, has_side_effects=True, vmem_limit_bytes=(64 << 20) - (12288 << 10)
         ),
     )(tokens.reshape(n_rows, width), routes.transpose(0, 2, 1), router, w_gate, w_up, w_down)
-    return dot_tn(mixing, values).astype(BF16).reshape(tokens.shape)
+    return out.reshape(tokens.shape)
 
 
 def spread(tokens, routes, router, w_gate, w_up, w_down):

time: 48.7 us -> 47.9 us (0.984)
  local copies, waits for them, and re-layouts: 0 us -> 2.56 us
  matrix products: 2.38 us -> 0 us
  Pallas kernels: 46 us -> 45.1 us
    unnamed x0 -> x5, local copies, waits for them, and re-layouts: none -> 2.56 us
    dot_general x1 -> x0, matrix products: 2.38 us -> none  [dot_tn(): lax.dot_general(a, b, (((0,), (0,)), ((), ())), preferred_element_type=F32)]
    pallas_call x1, Pallas kernels: 46 us -> 45.1 us  [fused(): pl.pallas_call(kernel, out_shape=jax.ShapeDtypeStruct((n_rows, width), BF...]
where the time goes in v4:
time: 47.9 us; the launch traced here: 47.7 us
  Pallas kernels  45.1 us (94%)
  local copies, waits for them, and re-layouts  2.56 us (5%)
    pallas_call x1, Pallas kernels, fused(): pl.pallas_call(kernel, out_shape=jax.ShapeDtypeStruct((n_rows, width), BF...  45.1 us
    unnamed x5, local copies, waits for them, and re-layouts  2.56 us

profile of v4, /device:TPU:1, one launch (start us, length us, event | category | flops | bytes accessed | tf_op | source)
XLA Modules:
  0.0 47.7 jit_solution(15125395172748128460)
XLA Ops:
  0.0 0.0 copy-start
  0.0 0.9 %copy-done = bf16[16,7168]{1,0:T(8,128)(2,1)S(1)} copy-done((bf16[16,7168]{1,0:T(8,128)(2,1)S(1)}, bf16[16,7168]{1,0:T(8,128)(2,1)}, u32[]{:S(2)}) %copy-start) | copy-done | bytes 229400
  0.9 0.0 copy-start.1
  0.9 0.7 %copy-done.1 = s32[2,32,8]{1,2,0:T(8,128)S(1)} copy-done((s32[2,32,8]{1,2,0:T(8,128)S(1)}, s32[2,32,8]{1,2,0:T(8,128)}, u32[]{:S(2)}) %copy-start.1) | copy-done | bytes 2072
  1.6 45.1 %shard_map.64 = bf16[64,7168]{1,0:T(8,128)(2,1)S(1)} custom-call(bf16[64,7168]{1,0:T(8,128)(2,1)} %bitcast.5, s32[2,8,32]{2,1,0:T(8,128)S(1)} %bitcast.4, bf16[16,7168]{1,0:T(8,128)(2,1)S(1)} %copy-done, bf16[7168,256]{1,0:T(8,128)(2,1)} %w_gate.1, bf16[7168,256]{1,0:T(8,128)(2,1)} %w_up.1, bf16[256,7168]{1,0:T(8,128)(2,1)} %w_down.1), custom_call_target="tpu_custom_call" | custom-call | tf_op jit(solution)/shard_map/pallas_call | solution.py:388
  46.7 0.9 %copy.8 = bf16[2,32,7168]{2,1,0:T(8,128)(2,1)} copy(bf16[2,32,7168]{2,1,0:T(8,128)(2,1)S(1)} %bitcast.3) | data formatting | bytes 1835008
Async XLA Ops:
  0.0 0.9 %copy-start = (bf16[16,7168]{1,0:T(8,128)(2,1)S(1)}, bf16[16,7168]{1,0:T(8,128)(2,1)}, u32[]{:S(2)}) copy-start(bf16[16,7168]{1,0:T(8,128)(2,1)} %router.1) | copy-start | bytes 688132
  0.9 0.7 %copy-start.1 = (s32[2,32,8]{1,2,0:T(8,128)S(1)}, s32[2,32,8]{1,2,0:T(8,128)}, u32[]{:S(2)}) copy-start(s32[2,32,8]{1,2,0:T(8,128)} %param.7) | copy-start | bytes 6148

commit v5 on v4

--- a/solution.py
+++ b/solution.py
@@ -32,8 +32,8 @@
 
 
 def kernel(
-    tokens_hbm, routes, router, w_gate, w_up, w_down, out,
-    tokens, values, gate_v, up_v, down_v, router_v, mine, theirs, rows, parts, from_x, from_up, from_down, sums,
+    tokens, routes, router, w_gate, w_up, w_down, out,
+    values, gate_v, up_v, down_v, router_v, mine, theirs, rows, parts, from_x, from_up, from_down, sums,
     total_v, total_peer, logit_out, logit_in, logit_peer,
     load_sem, peer_send, peer_recv, row_recv, row_up, row_down, row_x,
     log_send, log_recv, x_send, x_recv, up_send, up_recv, down_send, down_recv,
@@ -49,8 +49,6 @@
 
     own_router = pltpu.make_async_copy(router, router_v.at[pool], load_sem.at[3])
     own_router.start()
-    own_tokens = pltpu.make_async_copy(tokens_hbm, tokens, load_sem.at[4])
-    own_tokens.start()
     loads = [
         pltpu.make_async_copy(w_gate, gate_v, load_sem.at[0]),
         pltpu.make_async_copy(w_up, up_v, load_sem.at[1]),
@@ -85,10 +83,6 @@
         return jnp.concatenate([left, right], axis=0).astype(BF16)
 
     sel_own, sel_other = select(pool), select(1 - pool)
-    own_tokens.wait()
-    own_router.wait()
-    for load in loads:
-        load.start()
     for p in range(PIECES):
         mine[p] = in_slots(sel_other, p)
 
@@ -103,7 +97,7 @@
     peer_rows = [to_peer(mine.at[p], theirs.at[p], p) for p in range(PIECES)]
     for copy in peer_rows:
         copy.start()
-    peer_router = to_peer(router_v.at[pool], router_v.at[pool], 2 * PIECES)
+    peer_router = to_peer(router, router_v.at[pool], 2 * PIECES)
     peer_router.start()
 
     def row_copy(p, z, target, sems):
@@ -132,6 +126,8 @@
 
         row_copy(p, line, across, row_x).start()
 
+    for load in loads:
+        load.start()
     for d in range(1, LINE):
         for p in range(PIECES):
             @pl.when(line - d >= 0)
@@ -156,6 +152,7 @@
 
                 row_copy(p, z, across, row_x).start()
 
+    own_router.wait()
     peer_router.wait_recv()
     for load in loads:
         load.wait()
@@ -388,10 +385,9 @@
     out = pl.pallas_call(
         kernel,
         out_shape=jax.ShapeDtypeStruct((n_rows, width), BF16),
-        in_specs=[hbm, vmem, hbm, hbm, hbm, hbm],
+        in_specs=[vmem, vmem, vmem, hbm, hbm, hbm],
         out_specs=vmem,
         scratch_shapes=[
-            pltpu.VMEM((n_rows, width), BF16),
             pltpu.VMEM((32, width), BF16),
             pltpu.VMEM(w_gate.shape, BF16),
             pltpu.VMEM(w_up.shape, BF16),
@@ -410,7 +406,7 @@
             pltpu.VMEM((chips, 8, 128), F32),
             pltpu.VMEM((chips, 8, 128), F32),
             pltpu.VMEM((chips, 8, 128), F32),
-            dma((5,)), dma((2 * PIECES + 2,)), dma((2 * PIECES + 2,)), dma((PIECES, chips)),
+            dma((4,)), dma((2 * PIECES + 2,)), dma((2 * PIECES + 2,)), dma((PIECES, chips)),
             dma((PIECES, LINE)), dma((PIECES, LINE)), dma((PIECES, LINE)),
             dma((chips,)), dma((chips,)), dma((PIECES, LINE)), dma((PIECES, LINE)),
             dma((PIECES, LINE)), dma((PIECES, LINE)), dma((PIECES, LINE)), dma((PIECES, LINE)),

time: 47.9 us -> 49 us (1.023)
  Pallas kernels: 45.1 us -> 46.3 us
    pallas_call x1, Pallas kernels: 45.1 us -> 46.3 us  [fused(): pl.pallas_call(kernel, out_shape=jax.ShapeDtypeStruct((n_rows, width), BF...]
where the time goes in v5:
time: 49 us; the launch traced here: 48.8 us
  Pallas kernels  46.3 us (94%)
  local copies, waits for them, and re-layouts  2.56 us (5%)
    pallas_call x1, Pallas kernels, fused(): pl.pallas_call(kernel, out_shape=jax.ShapeDtypeStruct((n_rows, width), BF...  46.3 us
    unnamed x5, local copies, waits for them, and re-layouts  2.56 us

profile of v5, /device:TPU:1, one launch (start us, length us, event | category | flops | bytes accessed | tf_op | source)
XLA Modules:
  0.0 48.8 jit_solution(13544211969300686170)
XLA Ops:
  0.0 0.0 copy-start
  0.0 0.9 %copy-done = bf16[16,7168]{1,0:T(8,128)(2,1)S(1)} copy-done((bf16[16,7168]{1,0:T(8,128)(2,1)S(1)}, bf16[16,7168]{1,0:T(8,128)(2,1)}, u32[]{:S(2)}) %copy-start) | copy-done | bytes 229400
  0.9 0.0 copy-start.1
  0.9 0.7 %copy-done.1 = s32[2,32,8]{1,2,0:T(8,128)S(1)} copy-done((s32[2,32,8]{1,2,0:T(8,128)S(1)}, s32[2,32,8]{1,2,0:T(8,128)}, u32[]{:S(2)}) %copy-start.1) | copy-done | bytes 2072
  1.6 46.3 %shard_map.64 = bf16[64,7168]{1,0:T(8,128)(2,1)S(1)} custom-call(bf16[64,7168]{1,0:T(8,128)(2,1)} %bitcast.5, s32[2,8,32]{2,1,0:T(8,128)S(1)} %bitcast.4, bf16[16,7168]{1,0:T(8,128)(2,1)S(1)} %copy-done, bf16[7168,256]{1,0:T(8,128)(2,1)} %w_gate.1, bf16[7168,256]{1,0:T(8,128)(2,1)} %w_up.1, bf16[256,7168]{1,0:T(8,128)(2,1)} %w_down.1), custom_call_target="tpu_custom_call" | custom-call | tf_op jit(solution)/shard_map/pallas_call | solution.py:385
  47.9 0.9 %copy.8 = bf16[2,32,7168]{2,1,0:T(8,128)(2,1)} copy(bf16[2,32,7168]{2,1,0:T(8,128)(2,1)S(1)} %bitcast.3) | data formatting | bytes 1835008
Async XLA Ops:
  0.0 0.9 %copy-start = (bf16[16,7168]{1,0:T(8,128)(2,1)S(1)}, bf16[16,7168]{1,0:T(8,128)(2,1)}, u32[]{:S(2)}) copy-start(bf16[16,7168]{1,0:T(8,128)(2,1)} %router.1) | copy-start | bytes 688132
  0.9 0.7 %copy-start.1 = (s32[2,32,8]{1,2,0:T(8,128)S(1)}, s32[2,32,8]{1,2,0:T(8,128)}, u32[]{:S(2)}) copy-start(s32[2,32,8]{1,2,0:T(8,128)} %param.7) | copy-start | bytes 6148
